TPU v7x, 256 devices: a whole 4x4x8 slice. The times are simulated.
256 devices in a mesh: view: 16 (over y, z_hi), seq: 16 (over z_lo, x, core).
Axes of the slice: x: 4, y: 4, z: 8 (z_hi: 4, z_lo: 2; z = z_hi * 2 + z_lo), core: 2. Of those that a mesh axis runs over, the one named last changes fastest.
Arguments:
- tokens: bfloat16 [32768, 2048], P(('view', 'seq')), may hold values from -6 to 6
- w_qkv: bfloat16 [2048, 6144], P(None, 'seq'), may hold values from -0.125 to 0.125
- w_out: bfloat16 [2048, 2048], P('seq'), may hold values from -0.125 to 0.125
- mod_shift: float32 [16, 2048], P('view'), may hold values from -3 to 3
- mod_scale: float32 [16, 2048], P('view'), may hold values from -1 to 11
- mod_gate: float32 [16, 2048], P('view'), may hold values from -4 to 4
- partners: int32 [16, 6], P('view'), may hold values from 0 to 15, as said below
- partner_count: int32 [16], P('view'), may hold values from 2 to 6
Outputs:
- result: bfloat16 [32768, 2048], P(('view', 'seq'))
Inputs may be any that keep to these rules, and one draw needn't show every extreme that they name: partners[w, j] for j < partner_count[w] are distinct views other than w, each within 3 positions of w on the cyclic order of the 16 views; slots from partner_count[w] on hold w itself.
All inputs are finite; a program needn't handle non-finite values.
Results may differ from a plain program's by a relative error of at most 0.024.
The roundings to bfloat16 on the way count: a program that leaves them out, or rounds other values in their place, can miss the bound.
Values may be sent and summed in bfloat16 or wider, within the bound.
A program may use at most 64 MiB of HBM per device.

v0:
```python
import jax
import jax.numpy as jnp
from jax import lax
from jax.sharding import PartitionSpec as P

HEAD_DIM = 128
FRAME_TOK = 256


EPS = 1e-06


def from_behind(block, axis, distance):
    devices = range(lax.axis_size(axis))
    route = [((i - distance) % len(devices), i) for i in devices]
    return lax.ppermute(block, axis, route)


def view_attention(queries, keyval, extra_kv, flags, frame_tok):
    seq_len, head_count, head_width = queries.shape
    frames = seq_len // frame_tok
    score_scale = head_width ** (-0.5)
    key_part = keyval[:, :, 0]
    val_part = keyval[:, :, 1]

    def one_frame(frame_index):
        first_row = frame_index * frame_tok
        frame_q = lax.dynamic_slice_in_dim(queries, first_row, frame_tok, 0)
        far_kv = lax.dynamic_slice_in_dim(extra_kv, first_row, frame_tok, 1)
        own_scores = (
            jnp.einsum("qhe,khe->hqk", frame_q, key_part, preferred_element_type=jnp.float32)
            * score_scale
        )
        far_scores = (
            jnp.einsum(
                "qhe,pkhe->hqpk", frame_q, far_kv[:, :, :, 0], preferred_element_type=jnp.float32
            )
            * score_scale
        )
        far_scores = jnp.where(flags[None, None, :, None], far_scores, -jnp.inf)
        row_max = jnp.maximum(own_scores.max(axis=-1), far_scores.max(axis=(-2, -1)))
        own_prob = jnp.exp(own_scores - row_max[..., None])
        far_prob = jnp.exp(far_scores - row_max[..., None, None])
        weight_sum = own_prob.sum(axis=-1) + far_prob.sum(axis=(-2, -1))
        weighted = jnp.einsum(
            "hqk,khe->qhe",
            own_prob.astype(jnp.bfloat16),
            val_part,
            preferred_element_type=jnp.float32,
        )
        weighted = weighted + jnp.einsum(
            "hqpk,pkhe->qhe",
            far_prob.astype(jnp.bfloat16),
            far_kv[:, :, :, 1],
            preferred_element_type=jnp.float32,
        )
        return (weighted / jnp.transpose(weight_sum)[:, :, None]).astype(jnp.bfloat16)

    framed = lax.map(one_frame, jnp.arange(frames))
    return framed.reshape(seq_len, head_count * head_width)


def per_device(tokens, w_qkv, w_out, mod_shift, mod_scale, mod_gate, partners, partner_count):
    tokens_f32 = tokens.astype(jnp.float32)
    row_mean = jnp.mean(tokens_f32, axis=1, keepdims=True)
    centred = tokens_f32 - row_mean
    row_var = jnp.mean(centred * centred, axis=1, keepdims=True)
    normed = (centred * lax.rsqrt(row_var + EPS) * (1.0 + mod_scale) + mod_shift).astype(
        jnp.bfloat16
    )
    joined = jnp.dot(
        lax.all_gather(normed, "seq", axis=0, tiled=True), w_qkv, preferred_element_type=jnp.float32
    ).astype(jnp.bfloat16)
    seq_len = joined.shape[0]
    head_count = w_qkv.shape[1] // (3 * HEAD_DIM)
    joined = joined.reshape(seq_len, head_count, 3, HEAD_DIM)
    queries = joined[:, :, 0]
    keyval = joined[:, :, 1:]
    view_total = lax.axis_size("view")
    my_view = lax.axis_index("view")
    slot_ids = jnp.arange(partners.shape[1])
    received = []
    flag_list = []
    for offset in (1, -1, 2, -2, 3, -3):
        received.append(from_behind(keyval, "view", -offset))
        target = (my_view + offset) % view_total
        flag_list.append(jnp.any((partners[0] == target) & (slot_ids < partner_count[0])))
    extra_kv = jnp.stack(received)
    flags = jnp.stack(flag_list)
    attended = view_attention(queries, keyval, extra_kv, flags, FRAME_TOK)
    projected = lax.psum_scatter(
        jnp.dot(attended, w_out, preferred_element_type=jnp.float32).astype(jnp.bfloat16),
        "seq",
        scatter_dimension=0,
        tiled=True,
    ).astype(jnp.float32)
    return (tokens_f32 + mod_gate * projected).astype(jnp.bfloat16)


def solution(mesh):
    in_specs = (
        P(("view", "seq"), None),
        P(None, "seq"),
        P("seq", None),
        P("view", None),
        P("view", None),
        P("view", None),
        P("view", None),
        P("view"),
    )
    out_specs = P(("view", "seq"), None)
    return jax.shard_map(
        per_device, mesh=mesh, in_specs=in_specs, out_specs=out_specs, check_vma=False
    )
```

profile of v0, /device:TPU:2, one launch (start us, length us, event | category | flops | bytes accessed | tf_op | source)
XLA Modules:
  0.0 447.4 jit_solution(4814115101255749027)
XLA Ops:
  9.9 2.2 fusion.28
  12.2 57.6 %all-gather.2.cloned.1.call-done = bf16[2048,2048]{1,0:T(8,128)(2,1)} async-done(((bf16[128,2048]{1,0:T(8,128)(2,1)}), bf16[2048,2048]{1,0:T(8,128)(2,1)}) %all-gather.2.cloned.1.call-update) | async-done | bytes 8388624 | tf_op jit(solution)/shard_map/all_gather | solution.py:72
  69.8 6.8 %convolution_convert_fusion.1 = bf16[2048,384]{0,1:T(8,128)(2,1)S(1)} fusion(bf16[2048,2048]{1,0:T(8,128)(2,1)} %all-gather.2.cloned.1.call-done, bf16[2048,384]{1,0:T(8,128)(2,1)S(1)} %copy-done), kind=kOutput, calls=%fused_computation.30 | convolution fusion | flops 3222011904 | bytes 11534336 | tf_op jit(solution)/shard_map/dot_general | solution.py:71
  77.8 2.3 copy.39
  80.1 6.3 %collective-permute-start = (bf16[2048,1,2,128]{3,0,2,1:T(8,128)(2,1)}, bf16[2048,1,2,128]{3,0,2,1:T(8,128)(2,1)}, u32[]{:S(2)}, u32[]{:S(2)}) collective-permute-start(bf16[2048,1,2,128]{3,0,2,1:T(8,128)(2,1)} %copy.39), channel_id=1, source_target_pairs={{16,0},{32,16},{48,32},{64,48},{80,64},{96,80},{112,96},{128,112},... | collective-permute-start | bytes 3145736 | tf_op jit(solution)/shard_map/ppermute | solution.py:16
  87.9 3.7 stack.48
  91.7 4.6 %collective-permute-start.2 = (bf16[2048,1,2,128]{3,0,2,1:T(8,128)(2,1)}, bf16[2048,1,2,128]{3,0,2,1:T(8,128)(2,1)}, u32[]{:S(2)}, u32[]{:S(2)}) collective-permute-start(bf16[2048,1,2,128]{3,0,2,1:T(8,128)(2,1)} %copy.39), channel_id=1, source_target_pairs={{32,0},{48,16},{64,32},{80,48},{96,64},{112,80},{128,96},{144,112}... | collective-permute-start | bytes 3145736 | tf_op jit(solution)/shard_map/ppermute | solution.py:16
  97.7 2.7 collective-permute-start.4
  101.6 2.2 copy.37
  103.8 2.1 copy.38
  106.9 144.3 %collective-permute-done = bf16[2048,1,2,128]{3,0,2,1:T(8,128)(2,1)} collective-permute-done((bf16[2048,1,2,128]{3,0,2,1:T(8,128)(2,1)}, bf16[2048,1,2,128]{3,0,2,1:T(8,128)(2,1)}, u32[]{:S(2)}, u32[]{:S(2)}) %collective-permute-start) | collective-permute-done | bytes 1048608 | tf_op jit(solution)/shard_map/ppermute | solution.py:16
  251.2 2.6 collective-permute-start.5
  259.2 10.8 %collective-permute-done.4 = bf16[2048,1,2,128]{3,0,2,1:T(8,128)(2,1)} collective-permute-done((bf16[2048,1,2,128]{3,0,2,1:T(8,128)(2,1)}, bf16[2048,1,2,128]{3,0,2,1:T(8,128)(2,1)}, u32[]{:S(2)}, u32[]{:S(2)}) %collective-permute-start.4) | collective-permute-done | bytes 1048608 | tf_op jit(solution)/shard_map/ppermute | solution.py:16
  271.4 7.2 %collective-permute-done.5 = bf16[2048,1,2,128]{3,0,2,1:T(8,128)(2,1)S(1)} collective-permute-done((bf16[2048,1,2,128]{3,0,2,1:T(8,128)(2,1)S(1)}, bf16[2048,1,2,128]{3,0,2,1:T(8,128)(2,1)S(1)}, u32[]{:S(2)}, u32[]{:S(2)}) %collective-permute-start.5) | collective-permute-done | bytes 1048608 | tf_op jit(solution)/shard_map/ppermute | solution.py:16
  278.7 2.6 copy-done.5
  281.4 78.0 %while.10 = (s32[]{:T(128)}, bf16[8,256,1,128]{3,1,2,0:T(8,128)(2,1)}, s32[8]{0:T(128)S(1)}, bf16[2048,1,128]{2,0,1:T(8,128)(2,1)}, bf16[2048,1,128]{2,0,1:T(8,1...) while((s32[]{:T(128)}, ...), condition=%wide.region_13.14_spmd, body=%wide.region_8.13_spmd.sunk | while | flops 475758080 | bytes 32195368 | solution.py:59
  289.0 2.2 fusion.58
  297.0 1.6 convolution_bitcast_fusion.3
  298.7 2.2 fusion.58
  306.8 1.6 convolution_bitcast_fusion.3
  308.5 2.2 fusion.58
  316.5 1.6 convolution_bitcast_fusion.3
  318.2 2.2 fusion.58
  326.3 1.6 convolution_bitcast_fusion.3
  328.0 2.2 fusion.58
  336.0 1.6 convolution_bitcast_fusion.3
  337.7 2.2 fusion.58
  347.5 2.2 fusion.58
  357.2 2.2 fusion.58
  359.4 6.8 %convolution_convert_fusion = bf16[2048,2048]{1,0:T(8,128)(2,1)} fusion(bf16[2048,128]{1,0:T(8,128)(2,1)} %bitcast.152, bf16[128,2048]{1,0:T(8,128)(2,1)} %param.12), kind=kOutput, calls=%fused_computation.29 | convolution fusion | flops 1077936128 | bytes 9437184 | tf_op jit(solution)/shard_map/dot_general | solution.py:92
  366.2 72.4 %reduce-scatter.2.cloned.1.call-done = bf16[128,2048]{1,0:T(8,128)(2,1)} async-done(((bf16[2048,2048]{1,0:T(8,128)(2,1)}), bf16[128,2048]{1,0:T(8,128)(2,1)}) %reduce-scatter.2.cloned.1.call-update) | async-done | bytes 524304 | tf_op jit(solution)/shard_map/reduce_scatter | solution.py:91
  438.6 2.0 fusion.29
  (146 shorter events, 63.5 us)
Async XLA Ops:
  6.5 63.3 %copy-start = (bf16[2048,384]{1,0:T(8,128)(2,1)S(1)}, bf16[2048,384]{1,0:T(8,128)(2,1)}, u32[]{:S(2)}) copy-start(bf16[2048,384]{1,0:T(8,128)(2,1)} %param.11) | copy-start | bytes 4718596
  6.5 63.3 %all-gather.2.cloned.1.call-start = ((), (), s32[]{:S(2)}) async-start(), calls=%async_computation.1 | async-start | bytes 8912896 | tf_op jit(solution)/shard_map/all_gather | solution.py:72
  12.2 426.4 %reduce-scatter.2.cloned.1.call-start = ((), (), s32[]{:S(2)}) async-start(), calls=%async_computation.2 | async-start | bytes 8912896 | tf_op jit(solution)/shard_map/reduce_scatter | solution.py:91
  76.7 10.5 %copy-start.9 = (s32[1,6]{1,0:T(1,128)S(1)}, s32[1,6]{1,0:T(1,128)}, u32[]{:S(2)}) copy-start(s32[1,6]{1,0:T(1,128)} %param.16) | copy-start | bytes 76
  80.1 171.1 %collective-permute-start = (bf16[2048,1,2,128]{3,0,2,1:T(8,128)(2,1)}, bf16[2048,1,2,128]{3,0,2,1:T(8,128)(2,1)}, u32[]{:S(2)}, u32[]{:S(2)}) collective-permute-start(bf16[2048,1,2,128]{3,0,2,1:T(8,128)(2,1)} %copy.39), channel_id=1, source_target_pairs={{16,0},{32,16},{48,32},{64,48},{80,64},{96,80},{112,96},{128,112},... | collective-permute-start | bytes 3145736 | tf_op jit(solution)/shard_map/ppermute | solution.py:16
  87.1 168.0 %collective-permute-start.1 = (bf16[2048,1,2,128]{3,0,2,1:T(8,128)(2,1)}, bf16[2048,1,2,128]{3,0,2,1:T(8,128)(2,1)}, u32[]{:S(2)}, u32[]{:S(2)}) collective-permute-start(bf16[2048,1,2,128]{3,0,2,1:T(8,128)(2,1)} %copy.39), channel_id=1, source_target_pairs={{240,0},{0,16},{16,32},{32,48},{48,64},{64,80},{80,96},{96,112},{1... | collective-permute-start | bytes 3145736 | tf_op jit(solution)/shard_map/ppermute | solution.py:16
  91.7 164.7 %collective-permute-start.2 = (bf16[2048,1,2,128]{3,0,2,1:T(8,128)(2,1)}, bf16[2048,1,2,128]{3,0,2,1:T(8,128)(2,1)}, u32[]{:S(2)}, u32[]{:S(2)}) collective-permute-start(bf16[2048,1,2,128]{3,0,2,1:T(8,128)(2,1)} %copy.39), channel_id=1, source_target_pairs={{32,0},{48,16},{64,32},{80,48},{96,64},{112,80},{128,96},{144,112}... | collective-permute-start | bytes 3145736 | tf_op jit(solution)/shard_map/ppermute | solution.py:16
  96.2 161.6 %collective-permute-start.3 = (bf16[2048,1,2,128]{3,0,2,1:T(8,128)(2,1)}, bf16[2048,1,2,128]{3,0,2,1:T(8,128)(2,1)}, u32[]{:S(2)}, u32[]{:S(2)}) collective-permute-start(bf16[2048,1,2,128]{3,0,2,1:T(8,128)(2,1)} %copy.39), channel_id=1, source_target_pairs={{224,0},{240,16},{0,32},{16,48},{32,64},{48,80},{64,96},{80,112},{... | collective-permute-start | bytes 3145736 | tf_op jit(solution)/shard_map/ppermute | solution.py:16
  97.7 172.3 %collective-permute-start.4 = (bf16[2048,1,2,128]{3,0,2,1:T(8,128)(2,1)}, bf16[2048,1,2,128]{3,0,2,1:T(8,128)(2,1)}, u32[]{:S(2)}, u32[]{:S(2)}) collective-permute-start(bf16[2048,1,2,128]{3,0,2,1:T(8,128)(2,1)} %copy.39), channel_id=1, source_target_pairs={{48,0},{64,16},{80,32},{96,48},{112,64},{128,80},{144,96},{160,112... | collective-permute-start | bytes 3145736 | tf_op jit(solution)/shard_map/ppermute | solution.py:16
  101.6 4.3 copy-start.6
  101.6 149.6 %copy-start.7 = (bf16[2048,1,2,128]{3,0,2,1:T(8,128)(2,1)S(1)}, bf16[2048,1,2,128]{3,0,2,1:T(8,128)(2,1)}, u32[]{:S(2)}) copy-start(bf16[2048,1,2,128]{3,0,2,1:T(8,128)(2,1)} %copy.39) | copy-start | bytes 3145732
  251.2 27.4 %collective-permute-start.5 = (bf16[2048,1,2,128]{3,0,2,1:T(8,128)(2,1)S(1)}, bf16[2048,1,2,128]{3,0,2,1:T(8,128)(2,1)S(1)}, u32[]{:S(2)}, u32[]{:S(2)}) collective-permute-start(bf16[2048,1,2,128]{3,0,2,1:T(8,128)(2,1)S(1)} %copy-done.7), channel_id=1, source_target_pairs={{208,0},{224,16},{240,32},{0,48},{16,64},{32,80},{48,96},{64,112},... | collective-permute-start | bytes 3145736 | tf_op jit(solution)/shard_map/ppermute | solution.py:16
  278.7 2.7 copy-start.5
  282.6 1.5 copy-start.3
  287.3 1.7 copy-start.2
  292.3 1.5 copy-start.3
  297.0 1.7 copy-start.2
  302.1 1.5 copy-start.3
  305.0 1.4 copy-start.1
  306.8 1.7 copy-start.2
  311.8 1.5 copy-start.3
  316.5 1.7 copy-start.2
  321.6 1.5 copy-start.3
  326.3 1.7 copy-start.2
  331.3 1.5 copy-start.3
  336.0 1.7 copy-start.2
  341.1 1.5 copy-start.3
  345.8 1.7 copy-start.2
  350.8 1.5 copy-start.3
  355.5 1.7 copy-start.2
  366.2 72.4 %copy-start.4 = (bf16[128,2048]{1,0:T(8,128)(2,1)S(1)}, bf16[128,2048]{1,0:T(8,128)(2,1)}, u32[]{:S(2)}) copy-start(bf16[128,2048]{1,0:T(8,128)(2,1)} %param.10) | copy-start | bytes 1572868
  366.2 72.4 %copy-start.8 = (f32[1,2048]{1,0:T(1,128)S(1)}, f32[1,2048]{1,0:T(1,128)}, u32[]{:S(2)}) copy-start(f32[1,2048]{1,0:T(1,128)} %param.15) | copy-start | bytes 24580
  (7 other events, 9.5 us)
Sparse Core Ops, SparseCore 0:
  12.3 57.4 all-gather.1
  366.3 72.2 reduce-scatter.1
where the time goes:
time: 454 us; the launch traced here: 447 us
  waiting for transfers between devices  292 us (64%)
  matrix products  66.8 us (15%)
  local copies, waits for them, and re-layouts  37 us (8%)
  starting transfers between devices  17.7 us (4%)
  other arithmetic  14.2 us (3%)
  between operations  14.2 us (3%)
  loops' own time  5.11 us (1%)
    ppermute x6, waiting for transfers between devices, from_behind(): return lax.ppermute(block, axis, route)  162 us
    reduce_scatter x1, waiting for transfers between devices, per_device(): lax.psum_scatter(jnp.dot(attended, w_out, preferred_element_type=jnp.floa...  72.4 us
    all_gather x1, waiting for transfers between devices, per_device(): lax.all_gather(normed, 'seq', axis=0, tiled=True)  57.6 us
    ppermute x6, starting transfers between devices, from_behind(): return lax.ppermute(block, axis, route)  17.7 us
    dot_general x8, matrix products, one_frame(): jnp.einsum('hqk,khe->qhe', own_prob.astype(jnp.bfloat16), val_part, prefe...  17.4 us
    unnamed x23, local copies, waits for them, and re-layouts  17 us
    dot_general x8, matrix products, one_frame(): jnp.einsum('hqpk,pkhe->qhe', far_prob.astype(jnp.bfloat16), far_kv[:, :,...  12.8 us
    dot_general x8, matrix products, one_frame(): jnp.einsum('qhe,pkhe->hqpk', frame_q, far_kv[:, :, :, 0], preferred_eleme...  12.1 us
  transfers between devices with their start and end apart: 8, of which 5 were waited for; matrix products, arithmetic and copies ran while one was open for 4% of the time, Pallas kernels for 0%

commit v1 on v0

v1 whole, which is shorter than its diff:
```python
import functools

import jax
import jax.numpy as jnp
from jax import lax
from jax.experimental import pallas as pl
from jax.experimental.pallas import tpu as pltpu
from jax.sharding import PartitionSpec as P

HEAD_DIM = 128
FRAME_TOK = 256
D = 2048
EPS = 1e-06
NEG = -1e30
EXP_SCALE = HEAD_DIM ** (-0.5) * 1.4426950408889634
MESH = pl.DeviceIdType.MESH


def kernel(
    tok_ref,
    wq_ref,
    shift_ref,
    scale_ref,
    bias_ref,
    out_ref,
    normed,
    wbuf,
    biases,
    qbuf,
    kvw,
    kvx,
    abuf,
    attr,
    bias_s,
    bias_r,
    up_s,
    up_r,
    dn_s,
    dn_r,
    sib_s,
    sib_r,
    wx_s,
    wx_r,
    wy_s,
    wy_r,
    x_s,
    x_r,
    y_s,
    y_r,
    a_s,
    a_r,
    loc_s,
):
    w = lax.axis_index("view")
    s = lax.axis_index("seq")
    y, zh = w // 4, w % 4
    zl, x, c = s // 8, (s // 2) % 4, s % 2
    z = zh * 2 + zl

    def dev(x_, y_, z_, c_):
        return {"view": y_ * 4 + z_ // 2, "seq": (z_ % 2) * 8 + x_ * 2 + c_}

    def rcopy(src, dst, ss, rs, device):
        return pltpu.make_async_remote_copy(
            src_ref=src, dst_ref=dst, send_sem=ss, recv_sem=rs, device_id=device, device_id_type=MESH
        )

    def zdev(k, c_=None):
        return dev(x, y, (z + k) % 8, c if c_ is None else c_)

    def xdev(d):
        return dev((x + d) % 4, y, z, c)

    def ydev(d):
        return dev(x, (y + d) % 4, z, c)

    sib = dev(x, y, z, 1 - c)

    barrier = pltpu.get_barrier_semaphore()
    peers = [sib]
    for k in range(1, 8):
        peers += [zdev(k), zdev(k, 1 - c)]
    for d in range(1, 4):
        peers += [xdev(d), ydev(d)]
    for p in peers:
        pl.semaphore_signal(barrier, inc=1, device_id=p, device_id_type=MESH)

    t = tok_ref[...].astype(jnp.float32)
    t = t - jnp.mean(t, axis=1, keepdims=True)
    var = jnp.mean(t * t, axis=1, keepdims=True)
    normed[z, c] = (t * lax.rsqrt(var + EPS) * (1.0 + scale_ref[...]) + shift_ref[...]).astype(jnp.bfloat16)
    biases[zh] = bias_ref[...]

    pl.semaphore_wait(barrier, len(peers))

    quarter = wbuf.at[pl.ds(pl.multiple_of(y * 512, 512), 512)]
    my_quarter = wq_ref.at[pl.ds(pl.multiple_of(y * 512, 512), 512)]
    native = x == zh

    def wx_copy(d):
        return rcopy(my_quarter, quarter, wx_s.at[d - 1], wx_r, xdev(d))

    def wy_copy(d):
        return rcopy(quarter, quarter, wy_s.at[d - 1], wy_r.at[y], ydev(d))

    own_w = pltpu.make_async_copy(wq_ref, wbuf, loc_s)

    @pl.when(native)
    def _():
        for d in (1, 3, 2):
            wx_copy(d).start()
        own_w.start()

    def block(zz, cc, half):
        return normed.at[zz, cc, pl.ds(half * 64, 64)]

    def up_copy(k, half):
        b = block((z + 8 - k) % 8, c, half)
        return rcopy(b, b, up_s.at[k, half], up_r.at[k, half], zdev(1))

    def dn_copy(k, half):
        b = block((z + k) % 8, c, half)
        return rcopy(b, b, dn_s.at[k, half], dn_r.at[k, half], zdev(7))

    def sib_copy(k, half):
        b = block((z + k) % 8, c, half)
        return rcopy(b, b, sib_s.at[k, half], sib_r.at[k, half], sib)

    for half in (0, 1):
        up_copy(0, half).start()
        dn_copy(0, half).start()
    for half in (0, 1):
        sib_copy(0, half).start()

    def bias_copy(d):
        b = biases.at[zh]
        return rcopy(b, b, bias_s.at[d - 1], bias_r.at[d - 1], dev(x, y, (z + 2 * d) % 8, c))

    for d in range(1, 4):
        bias_copy(d).start()

    def event(k, half):
        if k < 4 or half == 0:
            up_copy(k - 1, half).wait_recv()
            if k < 3 or (k == 3 and half == 0):
                up_copy(k, half).start()
        if k < 4 or half == 1:
            dn_copy(k - 1, half).wait_recv()
            if k < 3 or (k == 3 and half == 1):
                dn_copy(k, half).start()
        if k < 4:
            sib_copy(8 - k, half).start()
            sib_copy(k, half).start()
        else:
            sib_copy(4, half).start()

    def x_copy(zz, d):
        v, fi = zz // 2, zz % 2
        return rcopy(kvw.at[fi, 3 + v], kvx.at[v, d - 1, fi], x_s.at[zz, d - 1], x_r.at[zz, d - 1], xdev(d))

    def yup_copy(zz):
        v, fi = zz // 2, zz % 2
        return rcopy(kvw.at[fi, 3 + v], kvw.at[fi, v - 1], y_s.at[zz, 0], y_r.at[fi, v - 1], ydev(1))

    def ydn_copy(zz):
        v, fi = zz // 2, zz % 2
        return rcopy(kvw.at[fi, 3 + v], kvw.at[fi, 7 + v], y_s.at[zz, 1], y_r.at[fi, 4 + v - 1], ydev(3))

    def unit(k):
        zz = (z + k) % 8
        for half in (0, 1):
            sib_copy(k, half).wait_recv()
        rows = normed[zz].reshape(256, D)
        joined = jnp.dot(rows, wbuf[...], preferred_element_type=jnp.float32).astype(jnp.bfloat16)
        qbuf[zz] = joined[:, :HEAD_DIM]
        kvw[zz % 2, 3 + zz // 2] = joined[:, HEAD_DIM:]
        for d in (1, 3, 2):
            x_copy(zz, d).start()

        @pl.when(zz >= 2)
        def _():
            yup_copy(zz).start()

        @pl.when(zz < 6)
        def _():
            ydn_copy(zz).start()

    event(1, 0)
    event(1, 1)

    @pl.when(jnp.logical_not(native))
    def _():
        wx_copy(1).wait_recv()
        for d in (1, 3, 2):
            wy_copy(d).start()

    event(2, 0)
    event(2, 1)

    @pl.when(native)
    def _():
        own_w.wait()

    @pl.when(jnp.logical_not(native))
    def _():
        for d in range(1, 4):
            q = (y + d) % 4
            rcopy(quarter, quarter, wy_s.at[0], wy_r.at[q], sib).wait_recv()

    unit(0)
    event(3, 0)
    unit(1)
    unit(7)
    event(3, 1)
    unit(2)
    unit(6)
    event(4, 0)
    event(4, 1)
    unit(3)
    unit(5)
    unit(4)

    def wait_unit(zz, carry):
        for d in range(1, 4):
            x_copy(zz, d).wait_recv()
        return carry

    lax.fori_loop(0, 8, wait_unit, 0)
    for fi in range(2):
        for slot in range(6):
            rcopy(kvw.at[fi, 0], kvw.at[fi, 0], y_s.at[0, 0], y_r.at[fi, slot], sib).wait_recv()
    for d in range(1, 4):
        bias_copy(d).wait_recv()

    head = zl * 8 + zh * 2 + c

    def a_copy(u, cc):
        return rcopy(
            abuf.at[u, pl.ds(cc * 128, 128)],
            attr.at[head],
            a_s.at[u, cc],
            a_r.at[head],
            dev(x, y, u, cc),
        )

    def attend(u, carry):
        v, fi = u // 2, u % 2
        q = qbuf[u]

        def score(kv):
            return lax.dot_general(
                q, kv[:, :HEAD_DIM], (((1,), (1,)), ((), ())), preferred_element_type=jnp.float32
            )

        kv_list = [kvw.at[1 - fi, 3 + v]]
        for d in range(3):
            for f in range(2):
                kv_list.append(kvx.at[v, d, f])
        for j in range(7):
            kv_list.append(kvw.at[fi, v + j])
        scores = []
        for i, kv in enumerate(kv_list):
            sc = score(kv)
            if i >= 7 and i != 10:
                row = biases[v, pl.ds(i - 7, 1), :]
                sc = sc + jnp.concatenate([row, row], axis=1)
            scores.append(sc)
        mx = functools.reduce(jnp.maximum, scores)
        mx = jnp.max(mx, axis=1, keepdims=True) * EXP_SCALE
        total = jnp.zeros((256, 256), jnp.float32)
        acc = jnp.zeros((256, HEAD_DIM), jnp.float32)
        for sc, kv in zip(scores, kv_list):
            p = jnp.exp2(sc * EXP_SCALE - mx)
            total = total + p
            acc = acc + jnp.dot(
                p.astype(jnp.bfloat16), kv[:, HEAD_DIM:], preferred_element_type=jnp.float32
            )
        den = jnp.sum(total, axis=1, keepdims=True)
        abuf[u] = (acc / den).astype(jnp.bfloat16)
        for cc in range(2):
            mine = jnp.logical_and(u == z, cc == c)

            @pl.when(mine)
            def _():
                attr[head] = abuf[u, pl.ds(cc * 128, 128)]

            @pl.when(jnp.logical_not(mine))
            def _():
                a_copy(u, cc).start()

        return carry

    lax.fori_loop(0, 8, attend, 0)

    for h in range(16):
        @pl.when(h != head)
        def _():
            rcopy(attr.at[h], attr.at[h], a_s.at[0, 0], a_r.at[h], sib).wait_recv()
        out_ref[:, h * 128 : (h + 1) * 128] = attr[h]

    for half in (0, 1):
        for k in range(3):
            up_copy(k, half).wait_send()
            dn_copy(k, half).wait_send()
        for k in range(8):
            if k != 4:
                sib_copy(k, half).wait_send()
    up_copy(3, 0).wait_send()
    dn_copy(3, 1).wait_send()
    for half in (0, 1):
        sib_copy(4, half).wait_send()
    for d in range(1, 4):
        bias_copy(d).wait_send()

    @pl.when(native)
    def _():
        for d in range(1, 4):
            wx_copy(d).wait_send()

    @pl.when(jnp.logical_not(native))
    def _():
        for d in range(1, 4):
            wy_copy(d).wait_send()

    def end_unit(zz, carry):
        for d in range(1, 4):
            x_copy(zz, d).wait_send()

        @pl.when(zz >= 2)
        def _():
            yup_copy(zz).wait_send()

        @pl.when(zz < 6)
        def _():
            ydn_copy(zz).wait_send()

        for cc in range(2):
            @pl.when(jnp.logical_not(jnp.logical_and(zz == z, cc == c)))
            def _():
                a_copy(zz, cc).wait_send()

        return carry

    lax.fori_loop(0, 8, end_unit, 0)


def per_device(tokens, w_qkv, w_out, mod_shift, mod_scale, mod_gate, partners, partner_count):
    me = lax.axis_index("view")
    views = lax.axis_size("view")
    w_full = lax.all_gather(w_out, "seq", axis=0, tiled=True)
    offset = jnp.arange(8) - 3
    target = (me + offset) % views
    used = jnp.arange(partners.shape[1])[None, :] < partner_count[0]
    flag = jnp.any((partners == target[:, None]) & used, axis=1)
    bias = jnp.broadcast_to(jnp.where(flag, 0.0, NEG)[:, None], (8, 128)).astype(jnp.float32)

    vmem = pl.BlockSpec(memory_space=pltpu.VMEM)
    bf16, f32 = jnp.bfloat16, jnp.float32
    dma = pltpu.SemaphoreType.DMA
    att = pl.pallas_call(
        kernel,
        out_shape=jax.ShapeDtypeStruct((128, D), bf16),
        in_specs=[vmem] * 5,
        out_specs=vmem,
        scratch_shapes=[
            pltpu.VMEM((8, 2, 128, D), bf16),
            pltpu.VMEM((D, 384), bf16),
            pltpu.VMEM((4, 8, 128), f32),
            pltpu.VMEM((8, 256, 128), bf16),
            pltpu.VMEM((2, 10, 256, 256), bf16),
            pltpu.VMEM((4, 3, 2, 256, 256), bf16),
            pltpu.VMEM((8, 256, 128), bf16),
            pltpu.VMEM((16, 128, 128), bf16),
            dma((3,)), dma((3,)),
            dma((4, 2)), dma((4, 2)),
            dma((4, 2)), dma((4, 2)),
            dma((8, 2)), dma((8, 2)),
            dma((3,)), dma,
            dma((3,)), dma((4,)),
            dma((8, 3)), dma((8, 3)),
            dma((8, 2)), dma((2, 6)),
            dma((8, 2)), dma((16,)),
            dma,
        ],
        compiler_params=pltpu.CompilerParams(
            collective_id=0, has_side_effects=True, vmem_limit_bytes=56 * 1024 * 1024
        ),
        cost_estimate=pl.CostEstimate(flops=8_000_000_000, bytes_accessed=30_000_000, transcendentals=7_000_000),
    )(tokens, w_qkv, mod_shift, mod_scale, bias)

    projected = jnp.dot(att, w_full, preferred_element_type=jnp.float32)
    return (tokens.astype(jnp.float32) + mod_gate * projected).astype(jnp.bfloat16)


def solution(mesh):
    in_specs = (
        P(("view", "seq"), None),
        P(None, "seq"),
        P("seq", None),
        P("view", None),
        P("view", None),
        P("view", None),
        P("view", None),
        P("view"),
    )
    out_specs = P(("view", "seq"), None)
    return jax.shard_map(
        per_device, mesh=mesh, in_specs=in_specs, out_specs=out_specs, check_vma=False
    )
```

time: 454 us -> 163 us (0.36); the launches traced: 447 us -> 161 us
  waiting for transfers between devices: 292 us -> 0.73 us
  Pallas kernels: 0 us -> 139 us
  matrix products: 66.8 us -> 5.65 us
  local copies, waits for them, and re-layouts: 37 us -> 0.67 us
  starting transfers between devices: 17.7 us -> 0.01 us
  other arithmetic: 14.2 us -> 0.87 us
  loops' own time: 5.11 us -> 0 us
    ppermute x6 -> x0, waiting for transfers between devices: 162 us -> none  [from_behind(): return lax.ppermute(block, axis, route)]
    pallas_call x0 -> x1, Pallas kernels: none -> 139 us  [per_device(): pl.pallas_call(kernel, out_shape=jax.ShapeDtypeStruct((128, D), bf16), in...]
    reduce_scatter x1 -> x0, waiting for transfers between devices: 72.4 us -> none  [per_device(): lax.psum_scatter(jnp.dot(attended, w_out, preferred_element_type=jnp.floa...]
    dot_general x34 -> x1, matrix products: 66.8 us -> 5.65 us  [per_device(): projected = jnp.dot(att, w_full, preferred_element_type=jnp.float32)]
    all_gather x1, waiting for transfers between devices: 57.6 us -> 0.02 us  [per_device(): w_full = lax.all_gather(w_out, 'seq', axis=0, tiled=True)]
    ppermute x6 -> x0, starting transfers between devices: 17.7 us -> none  [from_behind(): return lax.ppermute(block, axis, route)]
    unnamed x23 -> x4, local copies, waits for them, and re-layouts: 17 us -> 0.01 us
    while x48 -> x0, local copies, waits for them, and re-layouts: 9.17 us -> none
  transfers between devices with their start and end apart: 8 -> 1, of which waited for: 5 -> 0; matrix products, arithmetic and copies ran while one was open for 4% -> 1% of each run, Pallas kernels for 0% -> 86%
where the time goes in v1:
time: 163 us; the launch traced here: 161 us
  Pallas kernels  139 us (85%)
  between operations  14.1 us (9%)
  matrix products  5.65 us (3%)
    pallas_call x1, Pallas kernels, per_device(): pl.pallas_call(kernel, out_shape=jax.ShapeDtypeStruct((128, D), bf16), in...  139 us
    dot_general x1, matrix products, per_device(): projected = jnp.dot(att, w_full, preferred_element_type=jnp.float32)  5.65 us
  transfers between devices with their start and end apart: 1, of which 0 were waited for; matrix products, arithmetic and copies ran while one was open for 1% of the time, Pallas kernels for 86%

profile of v1, /device:TPU:2, one launch (start us, length us, event | category | flops | bytes accessed | tf_op | source)
XLA Modules:
  0.0 161.2 jit_solution(9181047554828431972)
XLA Ops:
  6.5 0.0 all-gather.2.cloned.1.call-start
  6.5 0.7 all-gather.2.cloned.1.call-update
  7.9 0.8 and_reduce_fusion
  8.8 0.7 broadcast_in_dim.18.bias_ref
  9.5 0.0 copy-start
  9.5 0.0 copy-start.1
  9.5 139.2 %shard_map.82 = bf16[128,2048]{1,0:T(8,128)(2,1)} custom-call(bf16[128,2048]{1,0:T(8,128)(2,1)} %tok_ref.1, bf16[2048,384]{1,0:T(8,128)(2,1)} %wq_ref.1, f32[1,2048]{1,0:T(1,128)} %shift_ref.1, f32[1,2048]{1,0:T(1,128)} %scale_ref.1, f32[8,128]{1,0:T(8,128)} %broadcast_in_dim.18.bias_ref), custom_call_target="tpu_custom_call" | custom-call | flops 8000000000 | bytes 30000000 | tf_op jit(solution)/shard_map/pallas_call | solution.py:360
  148.7 0.0 all-gather.2.cloned.1.call-done
  148.7 0.0 copy-done
  148.7 0.0 copy-done.1
  148.7 5.7 %fusion.1 = bf16[128,2048]{1,0:T(8,128)(2,1)} fusion(bf16[128,2048]{1,0:T(8,128)(2,1)} %shard_map.82, bf16[2048,2048]{1,0:T(8,128)(2,1)} %all-gather.2.cloned.1.call-done, bf16[128,2048]{1,0:T(8,128)(2,1)S(1)} %copy-done, f32[2048]{0:T(1024)S(1)} %bitcast.6), kind=kOutput, calls=%fused_computation.2 | convolution fusion | flops 1074790400 | bytes 9969664 | tf_op jit(solution)/shard_map/dot_general | solution.py:391
  (3 shorter events, 0.0 us)
Async XLA Ops:
  6.5 142.2 %all-gather.2.cloned.1.call-start = ((), (), s32[]{:S(2)}) async-start(), calls=%async_computation | async-start | bytes 8912896 | tf_op jit(solution)/shard_map/all_gather | solution.py:350
  9.5 139.3 %copy-start = (bf16[128,2048]{1,0:T(8,128)(2,1)S(1)}, bf16[128,2048]{1,0:T(8,128)(2,1)}, u32[]{:S(2)}) copy-start(bf16[128,2048]{1,0:T(8,128)(2,1)} %tok_ref.1) | copy-start | bytes 1572868
  9.5 139.3 %copy-start.1 = (f32[1,2048]{1,0:T(1,128)S(1)}, f32[1,2048]{1,0:T(1,128)}, u32[]{:S(2)}) copy-start(f32[1,2048]{1,0:T(1,128)} %param.13) | copy-start | bytes 24580
Sparse Core Ops, SparseCore 0:
  9.2 97.3 all-gather.1

commit v2 on v1

--- a/solution.py
+++ b/solution.py
@@ -19,8 +19,10 @@
 def kernel(
     tok_ref,
     wq_ref,
+    wo_ref,
     shift_ref,
     scale_ref,
+    gate_ref,
     bias_ref,
     out_ref,
     normed,
@@ -31,6 +33,7 @@
     kvx,
     abuf,
     attr,
+    wout,
     bias_s,
     bias_r,
     up_s,
@@ -45,10 +48,20 @@
     wy_r,
     x_s,
     x_r,
+    f_s,
+    f_r,
     y_s,
     y_r,
     a_s,
     a_r,
+    ox_s,
+    ox_r,
+    oy_s,
+    oy_r,
+    oz_s,
+    oz_r,
+    os_s,
+    os_r,
     loc_s,
 ):
     w = lax.axis_index("view")
@@ -93,22 +106,41 @@
 
     pl.semaphore_wait(barrier, len(peers))
 
-    quarter = wbuf.at[pl.ds(pl.multiple_of(y * 512, 512), 512)]
-    my_quarter = wq_ref.at[pl.ds(pl.multiple_of(y * 512, 512), 512)]
+    def piece(ref, p):
+        return ref.at[pl.ds(pl.multiple_of(y * 512, 512), 512), pl.ds(p * 128, 128)]
+
     native = x == zh
 
-    def wx_copy(d):
-        return rcopy(my_quarter, quarter, wx_s.at[d - 1], wx_r, xdev(d))
-
-    def wy_copy(d):
-        return rcopy(quarter, quarter, wy_s.at[d - 1], wy_r.at[y], ydev(d))
-
-    own_w = pltpu.make_async_copy(wq_ref, wbuf, loc_s)
+    def wx_copy(p, d):
+        return rcopy(piece(wq_ref, p), piece(wbuf, p), wx_s.at[p, d - 1], wx_r.at[p], xdev(d))
+
+    def wy_copy(p, d):
+        return rcopy(piece(wbuf, p), piece(wbuf, p), wy_s.at[p, d - 1], wy_r.at[p, y], ydev(d))
+
+    def pass_weights(p):
+        @pl.when(jnp.logical_not(native))
+        def _():
+            wx_copy(p, 1).wait_recv()
+            for d in (1, 3, 2):
+                wy_copy(p, d).start()
+
+    def wait_weights(p):
+        @pl.when(jnp.logical_not(native))
+        def _():
+            for d in range(1, 4):
+                rcopy(piece(wbuf, p), piece(wbuf, p), wy_s.at[p, 0], wy_r.at[p, (y + d) % 4], sib).wait_recv()
+
+    own_w = pltpu.make_async_copy(wq_ref, wbuf, loc_s.at[0])
+    own_o = pltpu.make_async_copy(
+        wo_ref, wout.at[c, zl, pl.ds(pl.multiple_of(x * 128, 128), 128)], loc_s.at[1]
+    )
+    own_o.start()
 
     @pl.when(native)
     def _():
-        for d in (1, 3, 2):
-            wx_copy(d).start()
+        for p in (1, 2, 0):
+            for d in (1, 3, 2):
+                wx_copy(p, d).start()
         own_w.start()
 
     def block(zz, cc, half):
@@ -158,6 +190,19 @@
         v, fi = zz // 2, zz % 2
         return rcopy(kvw.at[fi, 3 + v], kvx.at[v, d - 1, fi], x_s.at[zz, d - 1], x_r.at[zz, d - 1], xdev(d))
 
+    def f_copy(zz, half, direct):
+        v, fi = zz // 2, zz % 2
+        rows = pl.ds(half * 128, 128)
+        src = kvw.at[fi, 3 + v, rows] if direct else kvx.at[v, 2 * half, fi, rows]
+        to = xdev(2) if direct else xdev(1 + 2 * half)
+        return rcopy(src, kvx.at[v, 1, fi, rows], f_s.at[zz, half], f_r.at[zz, half], to)
+
+    def forward(k):
+        zz = (z + k) % 8
+        for half in (0, 1):
+            x_copy(zz, 1 + 2 * half).wait_recv()
+            f_copy(zz, half, False).start()
+
     def yup_copy(zz):
         v, fi = zz // 2, zz % 2
         return rcopy(kvw.at[fi, 3 + v], kvw.at[fi, v - 1], y_s.at[zz, 0], y_r.at[fi, v - 1], ydev(1))
@@ -166,16 +211,20 @@
         v, fi = zz // 2, zz % 2
         return rcopy(kvw.at[fi, 3 + v], kvw.at[fi, 7 + v], y_s.at[zz, 1], y_r.at[fi, 4 + v - 1], ydev(3))
 
-    def unit(k):
+    def rows_of(k):
+        return normed[(z + k) % 8].reshape(256, D)
+
+    def kv_unit(k):
         zz = (z + k) % 8
         for half in (0, 1):
             sib_copy(k, half).wait_recv()
-        rows = normed[zz].reshape(256, D)
-        joined = jnp.dot(rows, wbuf[...], preferred_element_type=jnp.float32).astype(jnp.bfloat16)
-        qbuf[zz] = joined[:, :HEAD_DIM]
-        kvw[zz % 2, 3 + zz // 2] = joined[:, HEAD_DIM:]
-        for d in (1, 3, 2):
+        kv = jnp.dot(rows_of(k), wbuf[:, HEAD_DIM:], preferred_element_type=jnp.float32)
+        kvw[zz % 2, 3 + zz // 2] = kv.astype(jnp.bfloat16)
+        for d in (1, 3):
             x_copy(zz, d).start()
+        if k == 4:
+            for half in (0, 1):
+                f_copy(zz, half, True).start()
 
         @pl.when(zz >= 2)
         def _():
@@ -185,44 +234,99 @@
         def _():
             ydn_copy(zz).start()
 
+    def q_unit(k):
+        q = jnp.dot(rows_of(k), wbuf[:, :HEAD_DIM], preferred_element_type=jnp.float32)
+        qbuf[(z + k) % 8] = q.astype(jnp.bfloat16)
+
+    par = y % 2
+
+    def wrows(xx, first, count):
+        return pl.ds(pl.multiple_of(xx * 128 + first, count), count)
+
+    def ox_copy(d):
+        return rcopy(
+            wo_ref.at[pl.ds(pl.multiple_of(par * 64, 64), 64)],
+            wout.at[c, zl, wrows(x, par * 64, 64)],
+            ox_s.at[d - 1],
+            ox_r.at[d - 1],
+            xdev(d),
+        )
+
+    def oy_copy(d, up):
+        b = wout.at[c, zl, wrows((x + d) % 4, par * 64 + (1 - up) * 32, 32)]
+        return rcopy(b, b, oy_s.at[d - 1, up], oy_r.at[d - 1, up], ydev(1 if up else 3))
+
+    def oz_copy(up):
+        b = wout.at[c, zl, pl.ds((1 - up) * 256, 256)]
+        return rcopy(b, b, oz_s.at[up], oz_r.at[up], zdev(1 if up else 7))
+
+    def os_copy(i):
+        b = wout.at[c, zl] if i == 2 else wout.at[c, 1 - zl, pl.ds((1 - i) * 256, 256)]
+        return rcopy(b, b, os_s.at[i], os_r.at[i], sib)
+
+    pass_weights(1)
     event(1, 0)
+    pass_weights(2)
     event(1, 1)
-
-    @pl.when(jnp.logical_not(native))
-    def _():
-        wx_copy(1).wait_recv()
-        for d in (1, 3, 2):
-            wy_copy(d).start()
-
+    pass_weights(0)
+    for d in (1, 3, 2):
+        ox_copy(d).start()
     event(2, 0)
-    event(2, 1)
 
     @pl.when(native)
     def _():
         own_w.wait()
 
-    @pl.when(jnp.logical_not(native))
-    def _():
-        for d in range(1, 4):
-            q = (y + d) % 4
-            rcopy(quarter, quarter, wy_s.at[0], wy_r.at[q], sib).wait_recv()
-
-    unit(0)
+    wait_weights(1)
+    wait_weights(2)
+    kv_unit(0)
+    kv_unit(1)
+    kv_unit(7)
+    event(2, 1)
+    kv_unit(2)
+    kv_unit(6)
+    wait_weights(0)
+    q_unit(0)
+    q_unit(1)
+    q_unit(7)
     event(3, 0)
-    unit(1)
-    unit(7)
+    forward(0)
+    for d in range(1, 4):
+        ox_copy(d).wait_recv()
+    for d in range(1, 4):
+        for up in (1, 0):
+            oy_copy(d, up).start()
+    q_unit(2)
+    q_unit(6)
     event(3, 1)
-    unit(2)
-    unit(6)
+    kv_unit(3)
+    kv_unit(5)
+    forward(1)
+    forward(7)
     event(4, 0)
     event(4, 1)
-    unit(3)
-    unit(5)
-    unit(4)
+    kv_unit(4)
+    own_o.wait()
+    for d in range(1, 4):
+        for up in (1, 0):
+            oy_copy(d, up).wait_recv()
+    for up in (1, 0):
+        oz_copy(up).start()
+    os_copy(2).start()
+    forward(2)
+    forward(6)
+    q_unit(3)
+    q_unit(5)
+    q_unit(4)
+    forward(3)
+    forward(5)
+
+    for half in (0, 1):
+        x_copy((z + 4) % 8, 1 + 2 * half).wait_recv()
 
     def wait_unit(zz, carry):
-        for d in range(1, 4):
-            x_copy(zz, d).wait_recv()
+        for half in (0, 1):
+            f_copy(zz, half, False).wait_recv()
         return carry
 
     lax.fori_loop(0, 8, wait_unit, 0)
@@ -234,10 +338,13 @@
 
     head = zl * 8 + zh * 2 + c
 
+    def acols(h):
+        return attr.at[(h % 2) * 2 + h // 8, :, pl.ds(pl.multiple_of((h // 2) % 4 * 128, 128), 128)]
+
     def a_copy(u, cc):
         return rcopy(
             abuf.at[u, pl.ds(cc * 128, 128)],
-            attr.at[head],
+            acols(head),
             a_s.at[u, cc],
             a_r.at[head],
             dev(x, y, u, cc),
@@ -282,7 +389,7 @@
 
             @pl.when(mine)
             def _():
-                attr[head] = abuf[u, pl.ds(cc * 128, 128)]
+                acols(head)[...] = abuf[u, pl.ds(cc * 128, 128)]
 
             @pl.when(jnp.logical_not(mine))
             def _():
@@ -292,11 +399,30 @@
 
     lax.fori_loop(0, 8, attend, 0)
 
+    for up in (1, 0):
+        oz_copy(up).wait_recv()
+        os_copy(up).start()
+    for i in range(3):
+        os_copy(i).wait_recv()
     for h in range(16):
         @pl.when(h != head)
         def _():
-            rcopy(attr.at[h], attr.at[h], a_s.at[0, 0], a_r.at[h], sib).wait_recv()
-        out_ref[:, h * 128 : (h + 1) * 128] = attr[h]
+            rcopy(acols(h), acols(h), a_s.at[0, 0], a_r.at[h], sib).wait_recv()
+
+    def project(j, carry):
+        cols = pl.ds(pl.multiple_of(j * 256, 256), 256)
+        acc = jnp.zeros((128, 256), jnp.float32)
+        for cc in range(2):
+            for ll in range(2):
+                acc = acc + jnp.dot(
+                    attr[cc * 2 + ll], wout[cc, ll, :, cols], preferred_element_type=jnp.float32
+                )
+        out_ref[:, cols] = (
+            tok_ref[:, cols].astype(jnp.float32) + gate_ref[:, cols] * acc
+        ).astype(jnp.bfloat16)
+        return carry
+
+    lax.fori_loop(0, 8, project, 0)
 
     for half in (0, 1):
         for k in range(3):
@@ -311,20 +437,30 @@
         sib_copy(4, half).wait_send()
     for d in range(1, 4):
         bias_copy(d).wait_send()
+        ox_copy(d).wait_send()
+        for up in (1, 0):
+            oy_copy(d, up).wait_send()
+    for up in (1, 0):
+        oz_copy(up).wait_send()
+    for i in range(3):
+        os_copy(i).wait_send()
 
     @pl.when(native)
     def _():
-        for d in range(1, 4):
-            wx_copy(d).wait_send()
+        for p in range(3):
+            for d in range(1, 4):
+                wx_copy(p, d).wait_send()
 
     @pl.when(jnp.logical_not(native))
     def _():
-        for d in range(1, 4):
-            wy_copy(d).wait_send()
+        for p in range(3):
+            for d in range(1, 4):
+                wy_copy(p, d).wait_send()
 
     def end_unit(zz, carry):
-        for d in range(1, 4):
-            x_copy(zz, d).wait_send()
+        for half in (0, 1):
+            x_copy(zz, 1 + 2 * half).wait_send()
+            f_copy(zz, half, False).wait_send()
 
         @pl.when(zz >= 2)
         def _():
@@ -347,7 +483,6 @@
 def per_device(tokens, w_qkv, w_out, mod_shift, mod_scale, mod_gate, partners, partner_count):
     me = lax.axis_index("view")
     views = lax.axis_size("view")
-    w_full = lax.all_gather(w_out, "seq", axis=0, tiled=True)
     offset = jnp.arange(8) - 3
     target = (me + offset) % views
     used = jnp.arange(partners.shape[1])[None, :] < partner_count[0]
@@ -357,10 +492,10 @@
     vmem = pl.BlockSpec(memory_space=pltpu.VMEM)
     bf16, f32 = jnp.bfloat16, jnp.float32
     dma = pltpu.SemaphoreType.DMA
-    att = pl.pallas_call(
+    return pl.pallas_call(
         kernel,
         out_shape=jax.ShapeDtypeStruct((128, D), bf16),
-        in_specs=[vmem] * 5,
+        in_specs=[vmem] * 7,
         out_specs=vmem,
         scratch_shapes=[
             pltpu.VMEM((8, 2, 128, D), bf16),
@@ -370,26 +505,29 @@
             pltpu.VMEM((2, 10, 256, 256), bf16),
             pltpu.VMEM((4, 3, 2, 256, 256), bf16),
             pltpu.VMEM((8, 256, 128), bf16),
-            pltpu.VMEM((16, 128, 128), bf16),
+            pltpu.VMEM((4, 128, 512), bf16),
+            pltpu.VMEM((2, 2, 512, D), bf16),
             dma((3,)), dma((3,)),
             dma((4, 2)), dma((4, 2)),
             dma((4, 2)), dma((4, 2)),
             dma((8, 2)), dma((8, 2)),
-            dma((3,)), dma,
-            dma((3,)), dma((4,)),
+            dma((3, 3)), dma((3,)),
+            dma((3, 3)), dma((3, 4)),
             dma((8, 3)), dma((8, 3)),
+            dma((8, 2)), dma((8, 2)),
             dma((8, 2)), dma((2, 6)),
             dma((8, 2)), dma((16,)),
-            dma,
+            dma((3,)), dma((3,)),
+            dma((3, 2)), dma((3, 2)),
+            dma((2,)), dma((2,)),
+            dma((3,)), dma((3,)),
+            dma((2,)),
         ],
         compiler_params=pltpu.CompilerParams(
             collective_id=0, has_side_effects=True, vmem_limit_bytes=56 * 1024 * 1024
         ),
         cost_estimate=pl.CostEstimate(flops=8_000_000_000, bytes_accessed=30_000_000, transcendentals=7_000_000),
-    )(tokens, w_qkv, mod_shift, mod_scale, bias)
-
-    projected = jnp.dot(att, w_full, preferred_element_type=jnp.float32)
-    return (tokens.astype(jnp.float32) + mod_gate * projected).astype(jnp.bfloat16)
+    )(tokens, w_qkv, w_out, mod_shift, mod_scale, mod_gate, bias)
 
 
 def solution(mesh):

time: 163 us -> 106 us (0.65)
  Pallas kernels: 139 us -> 100 us
  between operations: 14.1 us -> 0.67 us
  matrix products: 5.65 us -> 0 us
  local copies, waits for them, and re-layouts: 0.67 us -> 2.55 us
    pallas_call x1, Pallas kernels: 139 us -> 100 us  [per_device(): pl.pallas_call(kernel, out_shape=jax.ShapeDtypeStruct((128, D), bf16), in...]
    dot_general x1 -> x0, matrix products: 5.65 us -> none  [per_device(): projected = jnp.dot(att, w_full, preferred_element_type=jnp.float32)]
    unnamed x4 -> x1, local copies, waits for them, and re-layouts: 0.01 us -> 1.88 us
  transfers between devices with their start and end apart: 1 -> 0, of which waited for: 0 -> 0; matrix products, arithmetic and copies ran while one was open for 1% -> 0% of each run, Pallas kernels for 86% -> 0%
where the time goes in v2:
time: 106 us; the launch traced here: 104 us
  Pallas kernels  100 us (94%)
  local copies, waits for them, and re-layouts  2.55 us (2%)
    pallas_call x1, Pallas kernels, per_device(): pl.pallas_call(kernel, out_shape=jax.ShapeDtypeStruct((128, D), bf16), in...  100 us

profile of v2, /device:TPU:2, one launch (start us, length us, event | category | flops | bytes accessed | tf_op | source)
XLA Modules:
  0.0 104.2 jit_solution(3647432567371900677)
XLA Ops:
  0.7 0.8 and_reduce_fusion
  1.5 0.7 broadcast_in_dim.18.bias_ref
  2.2 100.1 %shard_map.82 = bf16[128,2048]{1,0:T(8,128)(2,1)} custom-call(bf16[128,2048]{1,0:T(8,128)(2,1)} %tok_ref.1, bf16[2048,384]{1,0:T(8,128)(2,1)} %wq_ref.1, bf16[128,2048]{1,0:T(8,128)(2,1)} %wo_ref.1, f32[1,2048]{1,0:T(1,128)} %shift_ref.1, f32[1,2048]{1,0:T(1,128)} %scale_ref.1, f32[1,2048]{1,0:T(1,128)} %gate_ref.1, f32[8,128]{1,0:T(8,128)} %broadcast_in_dim.18.bias_ref), custom_call_target="tpu_custom_call" | custom-call | flops 8000000000 | bytes 30000000 | tf_op jit(solution)/shard_map/pallas_call | solution.py:495
  102.3 1.9 %copy.11 = bf16[128,2048]{1,0:T(8,128)(2,1)} copy(bf16[128,2048]{1,0:T(8,128)(2,1)} %shard_map.82) | data formatting | bytes 1048576
  (3 shorter events, 0.0 us)

commit v3 on v2

v3 whole, which is shorter than its diff:
```python
import functools

import jax
import jax.numpy as jnp
from jax import lax
from jax.experimental import pallas as pl
from jax.experimental.pallas import tpu as pltpu
from jax.sharding import PartitionSpec as P

HEAD_DIM = 128
FRAME_TOK = 256
D = 2048
EPS = 1e-06
NEG = -1e30
EXP_SCALE = HEAD_DIM ** (-0.5) * 1.4426950408889634
MESH = pl.DeviceIdType.MESH


def kernel(
    tok_ref,
    wq_ref,
    wo_ref,
    shift_ref,
    scale_ref,
    gate_ref,
    partners_ref,
    count_ref,
    out_ref,
    normed,
    wbuf,
    biases,
    qbuf,
    kvw,
    kvx,
    abuf,
    attr,
    wout,
    m_st,
    l_st,
    acc_st,
    bias_s,
    bias_r,
    up_s,
    up_r,
    dn_s,
    dn_r,
    sib_s,
    sib_r,
    wx_s,
    wx_r,
    wy_s,
    wy_r,
    x_s,
    x_r,
    f_s,
    f_r,
    y_s,
    y_r,
    a_s,
    a_r,
    ox_s,
    ox_r,
    oy_s,
    oy_r,
    oz_s,
    oz_r,
    ow_s,
    ow_r,
    os_s,
    os_r,
    loc_s,
):
    w = lax.axis_index("view")
    s = lax.axis_index("seq")
    y, zh = lax.div(w, 4), lax.rem(w, 4)
    zl, x, c = lax.div(s, 8), lax.rem(lax.div(s, 2), 4), lax.rem(s, 2)
    z = zh * 2 + zl
    unit_z = [lax.rem(z + k, 8) for k in range(8)]
    unit_v = [lax.div(u, 2) for u in unit_z]
    unit_f = [lax.rem(u, 2) for u in unit_z]
    next_x = [lax.rem(x + d, 4) for d in range(4)]
    next_y = [lax.rem(y + d, 4) for d in range(4)]
    z_dev = [
        [{"view": y * 4 + v, "seq": f * 8 + x * 2 + cc} for cc in (c, 1 - c)]
        for v, f in zip(unit_v, unit_f)
    ]
    x_dev = [{"view": w, "seq": zl * 8 + xx * 2 + c} for xx in next_x]
    y_dev = [{"view": yy * 4 + zh, "seq": s} for yy in next_y]
    sib = z_dev[0][1]

    def rcopy(src, dst, ss, rs, device):
        return pltpu.make_async_remote_copy(
            src_ref=src, dst_ref=dst, send_sem=ss, recv_sem=rs, device_id=device, device_id_type=MESH
        )

    barrier = pltpu.get_barrier_semaphore()
    peers = [sib] + [p for k in range(1, 8) for p in z_dev[k]] + x_dev[1:] + y_dev[1:]
    for p in peers:
        pl.semaphore_signal(barrier, inc=1, device_id=p, device_id_type=MESH)

    t = tok_ref[...].astype(jnp.float32)
    t = t - jnp.mean(t, axis=1, keepdims=True)
    var = jnp.mean(t * t, axis=1, keepdims=True)
    normed[z, c] = (t * lax.rsqrt(var + EPS) * (1.0 + scale_ref[...]) + shift_ref[...]).astype(jnp.bfloat16)

    pl.semaphore_wait(barrier, len(peers))

    def block(zz, cc, half):
        return normed.at[zz, cc, pl.ds(half * 64, 64)]

    def up_copy(k, half):
        b = block(unit_z[(8 - k) % 8], c, half)
        return rcopy(b, b, up_s.at[k, half], up_r.at[k, half], z_dev[1][0])

    def dn_copy(k, half):
        b = block(unit_z[k], c, half)
        return rcopy(b, b, dn_s.at[k, half], dn_r.at[k, half], z_dev[7][0])

    def sib_copy(k, half):
        b = block(unit_z[k], c, half)
        return rcopy(b, b, sib_s.at[k, half], sib_r.at[k, half], sib)

    for half in (0, 1):
        up_copy(0, half).start()
        dn_copy(0, half).start()
    for half in (0, 1):
        sib_copy(0, half).start()

    def piece(ref, p):
        return ref.at[pl.ds(pl.multiple_of(y * 512, 512), 512), pl.ds(p * 128, 128)]

    native = x == zh

    def wx_copy(p, d):
        return rcopy(piece(wq_ref, p), piece(wbuf, p), wx_s.at[p, d - 1], wx_r.at[p], x_dev[d])

    def wy_copy(p, d):
        return rcopy(piece(wbuf, p), piece(wbuf, p), wy_s.at[p, d - 1], wy_r.at[p, y], y_dev[d])

    def pass_weights(p):
        @pl.when(jnp.logical_not(native))
        def _():
            wx_copy(p, 1).wait_recv()
            for d in (1, 3, 2):
                wy_copy(p, d).start()

    def wait_weights(p):
        @pl.when(jnp.logical_not(native))
        def _():
            for d in range(1, 4):
                rcopy(piece(wbuf, p), piece(wbuf, p), wy_s.at[p, 0], wy_r.at[p, next_y[d]], sib).wait_recv()

    own_w = pltpu.make_async_copy(wq_ref, wbuf, loc_s.at[0])
    own_o = pltpu.make_async_copy(wo_ref, wout.at[c, zl, x], loc_s.at[1])
    own_o.start()

    @pl.when(native)
    def _():
        for p in (1, 2, 0):
            for d in (1, 3, 2):
                wx_copy(p, d).start()
        own_w.start()

    for j in range(7):
        if j != 3:
            target = lax.rem(w + j + 13, 16)
            hits = 0.0
            for slot in range(6):
                hit = jnp.logical_and(partners_ref[0, slot] == target, count_ref[0] > slot)
                hits = hits + jnp.where(hit, 1.0, 0.0)
            biases[zh, j : j + 1, :] = jnp.full((1, 128), jnp.where(hits > 0.0, 0.0, NEG), jnp.float32)
    m_st[...] = jnp.full(m_st.shape, NEG, jnp.float32)
    l_st[...] = jnp.zeros(l_st.shape, jnp.float32)
    acc_st[...] = jnp.zeros(acc_st.shape, jnp.float32)

    def bias_copy(d):
        b = biases.at[zh]
        return rcopy(b, b, bias_s.at[d - 1], bias_r.at[d - 1], z_dev[2 * d][0])

    for d in range(1, 4):
        bias_copy(d).start()

    def event(k, half):
        if k < 4 or half == 0:
            up_copy(k - 1, half).wait_recv()
            if k < 3 or (k == 3 and half == 0):
                up_copy(k, half).start()
        if k < 4 or half == 1:
            dn_copy(k - 1, half).wait_recv()
            if k < 3 or (k == 3 and half == 1):
                dn_copy(k, half).start()
        if k < 4:
            sib_copy(8 - k, half).start()
            sib_copy(k, half).start()
        else:
            sib_copy(4, half).start()

    def x_copy(k, d):
        zz, v, fi = unit_z[k], unit_v[k], unit_f[k]
        return rcopy(kvw.at[fi, 3 + v], kvx.at[v, d - 1, fi], x_s.at[zz, d - 1], x_r.at[zz, d - 1], x_dev[d])

    def f_copy(k, half):
        zz, v, fi = unit_z[k], unit_v[k], unit_f[k]
        rows = pl.ds(half * 128, 128)
        src = kvw.at[fi, 3 + v, rows] if k == 4 else kvx.at[v, 2 * half, fi, rows]
        to = x_dev[2] if k == 4 else x_dev[1 + 2 * half]
        return rcopy(src, kvx.at[v, 1, fi, rows], f_s.at[zz, half], f_r.at[zz, half], to)

    def forward(k):
        for half in (0, 1):
            x_copy(k, 1 + 2 * half).wait_recv()
            f_copy(k, half).start()

    def yup_copy(k):
        zz, v, fi = unit_z[k], unit_v[k], unit_f[k]
        return rcopy(kvw.at[fi, 3 + v], kvw.at[fi, v - 1], y_s.at[zz, 0], y_r.at[fi, v - 1], y_dev[1])

    def ydn_copy(k):
        zz, v, fi = unit_z[k], unit_v[k], unit_f[k]
        return rcopy(kvw.at[fi, 3 + v], kvw.at[fi, 7 + v], y_s.at[zz, 1], y_r.at[fi, 3 + v], y_dev[3])

    def y_both(k, act):
        @pl.when(unit_z[k] >= 2)
        def _():
            act(yup_copy(k))

        @pl.when(unit_z[k] < 6)
        def _():
            act(ydn_copy(k))

    def kv_unit(k):
        for half in (0, 1):
            sib_copy(k, half).wait_recv()
        rows = normed[unit_z[k]].reshape(256, D)
        kv = jnp.dot(rows, wbuf[:, HEAD_DIM:], preferred_element_type=jnp.float32)
        kvw[unit_f[k], 3 + unit_v[k]] = kv.astype(jnp.bfloat16)
        for d in (1, 3):
            x_copy(k, d).start()
        if k == 4:
            for half in (0, 1):
                f_copy(k, half).start()
        y_both(k, lambda copy: copy.start())

    def q_unit(k):
        rows = normed[unit_z[k]].reshape(256, D)
        q = jnp.dot(rows, wbuf[:, :HEAD_DIM], preferred_element_type=jnp.float32)
        qbuf[unit_z[k]] = q.astype(jnp.bfloat16)

    par = lax.rem(y, 2)
    half_rows = pl.ds(pl.multiple_of(par * 64, 64), 64)

    def quarter_rows(up):
        return pl.ds(pl.multiple_of(par * 64 + (1 - up) * 32, 32), 32)

    def ox_copy(d):
        return rcopy(
            wo_ref.at[half_rows], wout.at[c, zl, x, half_rows], ox_s.at[d - 1], ox_r.at[d - 1], x_dev[d]
        )

    def oy_copy(d, up):
        b = wout.at[c, zl, next_x[d], quarter_rows(up)]
        return rcopy(b, b, oy_s.at[d - 1, up], oy_r.at[d - 1, up], y_dev[1 if up else 3])

    def drain_w_out():
        for d in range(1, 4):
            ox_copy(d).wait_send()
            for up in (1, 0):
                oy_copy(d, up).wait_send()

    def oz_copy(up):
        b = wout.at[c, zl, pl.ds((1 - up) * 2, 2), half_rows]
        return rcopy(b, b, oz_s.at[up], oz_r.at[up], z_dev[1 if up else 7][0])

    def ow_copy(pair, up):
        b = wout.at[c, 1 - zl, pl.ds(pair * 2, 2), quarter_rows(up)]
        return rcopy(b, b, ow_s.at[pair, up], ow_r.at[pair, up], y_dev[1 if up else 3])

    def os_copy(i):
        b = wout.at[c, zl] if i == 2 else wout.at[c, 1 - zl, pl.ds(i * 2, 2)]
        return rcopy(b, b, os_s.at[i], os_r.at[i], sib)

    @pl.when(jnp.logical_not(native))
    def _():
        for d in (1, 3, 2):
            ox_copy(d).start()

    pass_weights(1)
    event(1, 0)
    pass_weights(2)
    event(1, 1)
    pass_weights(0)

    @pl.when(native)
    def _():
        for p in range(3):
            for d in range(1, 4):
                wx_copy(p, d).wait_send()
        for d in (1, 3, 2):
            ox_copy(d).start()
        own_w.wait()

    def acols(cc, ll, xx):
        return attr.at[cc * 2 + ll, :, pl.ds(pl.multiple_of(xx * 128, 128), 128)]

    def a_copy(k, other):
        cc = 1 - c if other else c
        return rcopy(
            abuf.at[unit_z[k], pl.ds(pl.multiple_of(cc * 128, 128), 128)],
            acols(c, zl, zh),
            a_s.at[k, other],
            a_r.at[k, other],
            z_dev[k][other],
        )

    def a_wait(k, other):
        src = acols(1 - c if other else c, unit_f[(8 - k) % 8], unit_v[(8 - k) % 8])
        return rcopy(src, src, a_s.at[k, other], a_r.at[k, other], sib)

    def finish(ks):
        for k in ks:
            u = unit_z[k]
            den = jnp.sum(l_st[u], axis=1, keepdims=True)
            abuf[u] = (acc_st[u] / den).astype(jnp.bfloat16)
        for k in ks:
            if k == 0:
                acols(c, zl, zh)[...] = abuf[z, pl.ds(pl.multiple_of(c * 128, 128), 128)]
            else:
                a_copy(k, 0).start()
            a_copy(k, 1).start()

    def groups(parts):
        first = []
        for u, blocks in parts:
            q = qbuf[u]
            scores = []
            for kv, row in blocks:
                sc = lax.dot_general(
                    q, kv[:, :HEAD_DIM], (((1,), (1,)), ((), ())), preferred_element_type=jnp.float32
                )
                if row is not None:
                    b = biases[lax.div(u, 2), pl.ds(row, 1), :]
                    sc = sc + jnp.concatenate([b, b], axis=1)
                scores.append(sc)
            mx = functools.reduce(jnp.maximum, scores)
            mx = jnp.max(mx, axis=1, keepdims=True) * EXP_SCALE
            m_old = m_st[u]
            m_new = jnp.maximum(m_old, mx)
            first.append((scores, m_new, jnp.exp2(m_old - m_new)))
        second = []
        for (u, blocks), (scores, m_new, alpha) in zip(parts, first):
            m_two = jnp.concatenate([m_new, m_new], axis=1)
            total = jnp.zeros((256, 256), jnp.float32)
            acc = jnp.zeros((256, HEAD_DIM), jnp.float32)
            for sc, (kv, row) in zip(scores, blocks):
                p = jnp.exp2(sc * EXP_SCALE - m_two)
                total = total + p
                acc = acc + jnp.dot(
                    p.astype(jnp.bfloat16), kv[:, HEAD_DIM:], preferred_element_type=jnp.float32
                )
            second.append((total, acc))
        for (u, blocks), (scores, m_new, alpha), (total, acc) in zip(parts, first, second):
            m_st[u] = m_new
            l_st[u] = l_st[u] * alpha + total[:, :128] + total[:, 128:]
            acc_st[u] = acc_st[u] * alpha + acc

    def own_view(v):
        parts = []
        for fi in range(2):
            blocks = [(kvw.at[fi, 3 + v], None), (kvw.at[1 - fi, 3 + v], None)]
            blocks += [(kvx.at[v, d, f], None) for d in range(3) for f in range(2)]
            parts.append((2 * v + fi, blocks))
        groups(parts)

    def window(v, fi, deltas):
        blocks = [(kvw.at[fi, v + o], o) for delta in deltas for o in (delta - 1, delta + 3)]
        return 2 * v + fi, blocks

    def wait_x(k):
        for half in (0, 1):
            f_copy(k, half).wait_recv()
        if k == 4:
            for half in (0, 1):
                x_copy(k, 1 + 2 * half).wait_recv()

    def wait_y(k):
        y_both(k, lambda copy: copy.wait_recv())

    sign = 1 - 2 * zl
    view_b, view_c, view_d = lax.rem(zh + 4 - sign, 4), lax.rem(zh + 4 + sign, 4), unit_v[4]
    views = [unit_v[6], zh, unit_v[2]]
    gaps = [3, 2, 1]

    wait_weights(1)
    wait_weights(2)
    kv_unit(0)
    event(2, 0)
    kv_unit(1)
    kv_unit(7)
    wait_weights(0)
    event(2, 1)
    kv_unit(2)
    kv_unit(6)
    for k in (0, 1, 7):
        q_unit(k)
    forward(0)
    event(3, 0)
    for d in range(1, 4):
        ox_copy(d).wait_recv()
    for d in range(1, 4):
        for up in (1, 0):
            oy_copy(d, up).start()
    q_unit(2)
    q_unit(6)
    forward(1)
    forward(7)
    for half in (0, 1):
        for k in range(2):
            up_copy(k, half).wait_send()
            dn_copy(k, half).wait_send()
        for k in (0, 1, 7):
            sib_copy(k, half).wait_send()
    for d in range(1, 4):
        bias_copy(d).wait_send()
        bias_copy(d).wait_recv()

    @pl.when(jnp.logical_not(native))
    def _():
        for p in range(3):
            for d in range(1, 4):
                wy_copy(p, d).wait_send()

    event(3, 1)
    kv_unit(3)
    kv_unit(5)
    q_unit(3)
    q_unit(5)
    forward(2)
    forward(6)
    for d in range(1, 4):
        for up in (1, 0):
            oy_copy(d, up).wait_recv()
    own_o.wait()
    for up in (1, 0):
        oz_copy(up).start()
    for k in (0, 1, 7):
        wait_x(k)
    own_view(zh)
    for k in (0, 1, 7):
        for half in (0, 1):
            x_copy(k, 1 + 2 * half).wait_send()
            f_copy(k, half).wait_send()
        y_both(k, lambda copy: copy.wait_send())
    event(4, 0)
    event(4, 1)
    kv_unit(4)
    forward(3)
    forward(5)
    q_unit(4)
    os_copy(2).start()
    wait_x(2)
    wait_x(6)
    own_view(view_b)
    for k in (1, 7, 3, 5):
        wait_y(k)
    groups([window(unit_v[k], 1 - zl, (1, 2, 3)) for k in (1, 3, 5, 7)])
    finish((1, 7))
    for k in (0, 2, 6):
        wait_y(k)
    groups([window(v, zl, [e for e in (1, 2, 3) if e != g]) for v, g in zip(views, gaps)])
    for pair in (0, 1):
        oz_copy(1 - pair).wait_recv()
        for up in (1, 0):
            ow_copy(pair, up).start()
    wait_y(4)
    groups(
        [window(v, zl, (g,)) for v, g in zip(views, gaps)] + [window(view_d, zl, (1, 2, 3))]
    )
    wait_x(3)
    wait_x(5)
    own_view(view_c)
    finish((0, 2, 6))

    @pl.when(zl == 0)
    def _():
        finish((3,))

    @pl.when(zl == 1)
    def _():
        finish((5,))

    wait_x(4)
    own_view(view_d)

    @pl.when(zl == 0)
    def _():
        finish((5,))

    @pl.when(zl == 1)
    def _():
        finish((3,))

    finish((4,))

    for half in (0, 1):
        up_copy(2, half).wait_send()
        dn_copy(2, half).wait_send()
        for k in range(2, 7):
            sib_copy(k, half).wait_send()
    up_copy(3, 0).wait_send()
    dn_copy(3, 1).wait_send()
    drain_w_out()
    for k in (2, 3, 4, 5, 6):
        for half in (0, 1):
            x_copy(k, 1 + 2 * half).wait_send()
            f_copy(k, half).wait_send()
        y_both(k, lambda copy: copy.wait_send())

    for pair in (0, 1):
        for up in (1, 0):
            ow_copy(pair, up).wait_recv()
        os_copy(pair).start()
    for i in range(3):
        os_copy(i).wait_recv()
    for k in range(8):
        for other in (0, 1):
            if k or other:
                a_wait(k, other).wait_recv()

    for j in range(4):
        cols = pl.ds(j * 512, 512)
        acc = jnp.zeros((128, 512), jnp.float32)
        for cc in range(2):
            for ll in range(2):
                part = wout[cc, ll, :, :, cols].reshape(512, 512)
                acc = acc + jnp.dot(attr[cc * 2 + ll], part, preferred_element_type=jnp.float32)
        out_ref[:, cols] = (
            tok_ref[:, cols].astype(jnp.float32) + gate_ref[:, cols] * acc
        ).astype(jnp.bfloat16)

    for up in (1, 0):
        oz_copy(up).wait_send()
        for pair in (0, 1):
            ow_copy(pair, up).wait_send()
    for i in range(3):
        os_copy(i).wait_send()
    for k in range(8):
        for other in (0, 1):
            if k or other:
                a_copy(k, other).wait_send()


def per_device(tokens, w_qkv, w_out, mod_shift, mod_scale, mod_gate, partners, partner_count):
    vmem = pl.BlockSpec(memory_space=pltpu.VMEM)
    smem = pl.BlockSpec(memory_space=pltpu.SMEM)
    hbm = pl.BlockSpec(memory_space=pl.ANY)
    bf16, f32 = jnp.bfloat16, jnp.float32
    dma = pltpu.SemaphoreType.DMA
    return pl.pallas_call(
        kernel,
        out_shape=jax.ShapeDtypeStruct((128, D), bf16),
        in_specs=[vmem, hbm, hbm, vmem, vmem, vmem, smem, smem],
        out_specs=vmem,
        scratch_shapes=[
            pltpu.VMEM((8, 2, 128, D), bf16),
            pltpu.VMEM((D, 384), bf16),
            pltpu.VMEM((4, 8, 128), f32),
            pltpu.VMEM((8, 256, 128), bf16),
            pltpu.VMEM((2, 10, 256, 256), bf16),
            pltpu.VMEM((4, 3, 2, 256, 256), bf16),
            pltpu.VMEM((8, 256, 128), bf16),
            pltpu.VMEM((4, 128, 512), bf16),
            pltpu.VMEM((2, 2, 4, 128, D), bf16),
            pltpu.VMEM((8, 256, 128), f32),
            pltpu.VMEM((8, 256, 128), f32),
            pltpu.VMEM((8, 256, 128), f32),
            dma((3,)), dma((3,)),
            dma((4, 2)), dma((4, 2)),
            dma((4, 2)), dma((4, 2)),
            dma((8, 2)), dma((8, 2)),
            dma((3, 3)), dma((3,)),
            dma((3, 3)), dma((3, 4)),
            dma((8, 3)), dma((8, 3)),
            dma((8, 2)), dma((8, 2)),
            dma((8, 2)), dma((2, 6)),
            dma((8, 2)), dma((8, 2)),
            dma((3,)), dma((3,)),
            dma((3, 2)), dma((3, 2)),
            dma((2,)), dma((2,)),
            dma((2, 2)), dma((2, 2)),
            dma((3,)), dma((3,)),
            dma((2,)),
        ],
        compiler_params=pltpu.CompilerParams(
            collective_id=0, has_side_effects=True, vmem_limit_bytes=56 * 1024 * 1024
        ),
        cost_estimate=pl.CostEstimate(flops=8_000_000_000, bytes_accessed=30_000_000, transcendentals=7_000_000),
    )(tokens, w_qkv, w_out, mod_shift, mod_scale, mod_gate, partners, partner_count)


def solution(mesh):
    in_specs = (
        P(("view", "seq"), None),
        P(None, "seq"),
        P("seq", None),
        P("view", None),
        P("view", None),
        P("view", None),
        P("view", None),
        P("view"),
    )
    out_specs = P(("view", "seq"), None)
    return jax.shard_map(
        per_device, mesh=mesh, in_specs=in_specs, out_specs=out_specs, check_vma=False
    )
```

time: 106 us -> 96.1 us (0.907); the launches traced: 104 us -> 95.9 us
  Pallas kernels: 100 us -> 93.4 us
    pallas_call x1, Pallas kernels: 100 us -> 93.4 us  [per_device(): pl.pallas_call(kernel, out_shape=jax.ShapeDtypeStruct((128, D), bf16), in...]
where the time goes in v3:
time: 96.1 us; the launch traced here: 95.9 us
  Pallas kernels  93.4 us (97%)
  local copies, waits for them, and re-layouts  1.88 us (2%)
    pallas_call x1, Pallas kernels, per_device(): pl.pallas_call(kernel, out_shape=jax.ShapeDtypeStruct((128, D), bf16), in...  93.4 us

profile of v3, /device:TPU:2, one launch (start us, length us, event | category | flops | bytes accessed | tf_op | source)
XLA Modules:
  0.0 95.9 jit_solution(1479622099551097655)
XLA Ops:
  0.7 93.4 %shard_map.82 = bf16[128,2048]{1,0:T(8,128)(2,1)} custom-call(bf16[128,2048]{1,0:T(8,128)(2,1)} %tok_ref.1, bf16[2048,384]{1,0:T(8,128)(2,1)} %wq_ref.1, bf16[128,2048]{1,0:T(8,128)(2,1)} %wo_ref.1, f32[1,2048]{1,0:T(1,128)} %shift_ref.1, f32[1,2048]{1,0:T(1,128)} %scale_ref.1, f32[1,2048]{1,0:T(1,128)} %gate_ref.1, s32[1,6]{1,0:T(1,128)} %partners_ref.1, ...), custom_call_target="tpu_custom_call" | custom-call | flops 8000000000 | bytes 30000000 | tf_op jit(solution)/shard_map/pallas_call | solution.py:558
  94.0 1.9 %copy.11 = bf16[128,2048]{1,0:T(8,128)(2,1)} copy(bf16[128,2048]{1,0:T(8,128)(2,1)} %shard_map.82) | data formatting | bytes 1048576

commit v4 on v3

--- a/solution.py
+++ b/solution.py
@@ -279,11 +279,8 @@
         b = wout.at[c, zl] if i == 2 else wout.at[c, 1 - zl, pl.ds(i * 2, 2)]
         return rcopy(b, b, os_s.at[i], os_r.at[i], sib)
 
-    @pl.when(jnp.logical_not(native))
-    def _():
-        for d in (1, 3, 2):
-            ox_copy(d).start()
-
+    for d in (1, 3, 2):
+        ox_copy(d).start()
     pass_weights(1)
     event(1, 0)
     pass_weights(2)
@@ -295,8 +292,6 @@
         for p in range(3):
             for d in range(1, 4):
                 wx_copy(p, d).wait_send()
-        for d in (1, 3, 2):
-            ox_copy(d).start()
         own_w.wait()
 
     def acols(cc, ll, xx):
@@ -371,6 +366,15 @@
             parts.append((2 * v + fi, blocks))
         groups(parts)
 
+    def last_view(late):
+        parts = []
+        for fi in range(2):
+            blocks = [(kvx.at[view_d, d, zl if late else 1 - zl], None) for d in range(3)]
+            if not late:
+                blocks += [(kvw.at[fi, 3 + view_d], None), (kvw.at[1 - fi, 3 + view_d], None)]
+            parts.append((2 * view_d + fi, blocks))
+        groups(parts)
+
     def window(v, fi, deltas):
         blocks = [(kvw.at[fi, v + o], o) for delta in deltas for o in (delta - 1, delta + 3)]
         return 2 * v + fi, blocks
@@ -397,6 +401,11 @@
     kv_unit(1)
     kv_unit(7)
     wait_weights(0)
+    for d in range(1, 4):
+        ox_copy(d).wait_recv()
+    for d in range(1, 4):
+        for up in (1, 0):
+            oy_copy(d, up).start()
     event(2, 1)
     kv_unit(2)
     kv_unit(6)
@@ -404,11 +413,6 @@
         q_unit(k)
     forward(0)
     event(3, 0)
-    for d in range(1, 4):
-        ox_copy(d).wait_recv()
-    for d in range(1, 4):
-        for up in (1, 0):
-            oy_copy(d, up).start()
     q_unit(2)
     q_unit(6)
     forward(1)
@@ -430,18 +434,18 @@
                 wy_copy(p, d).wait_send()
 
     event(3, 1)
+    for d in range(1, 4):
+        for up in (1, 0):
+            oy_copy(d, up).wait_recv()
+    own_o.wait()
+    for up in (1, 0):
+        oz_copy(up).start()
     kv_unit(3)
     kv_unit(5)
     q_unit(3)
     q_unit(5)
     forward(2)
     forward(6)
-    for d in range(1, 4):
-        for up in (1, 0):
-            oy_copy(d, up).wait_recv()
-    own_o.wait()
-    for up in (1, 0):
-        oz_copy(up).start()
     for k in (0, 1, 7):
         wait_x(k)
     own_view(zh)
@@ -460,6 +464,10 @@
     wait_x(2)
     wait_x(6)
     own_view(view_b)
+    for pair in (0, 1):
+        oz_copy(1 - pair).wait_recv()
+        for up in (1, 0):
+            ow_copy(pair, up).start()
     for k in (1, 7, 3, 5):
         wait_y(k)
     groups([window(unit_v[k], 1 - zl, (1, 2, 3)) for k in (1, 3, 5, 7)])
@@ -467,10 +475,6 @@
     for k in (0, 2, 6):
         wait_y(k)
     groups([window(v, zl, [e for e in (1, 2, 3) if e != g]) for v, g in zip(views, gaps)])
-    for pair in (0, 1):
-        oz_copy(1 - pair).wait_recv()
-        for up in (1, 0):
-            ow_copy(pair, up).start()
     wait_y(4)
     groups(
         [window(v, zl, (g,)) for v, g in zip(views, gaps)] + [window(view_d, zl, (1, 2, 3))]
@@ -488,8 +492,9 @@
     def _():
         finish((5,))
 
+    last_view(False)
     wait_x(4)
-    own_view(view_d)
+    last_view(True)
 
     @pl.when(zl == 0)
     def _():

time: 96.1 us -> 95.4 us (level)
  Pallas kernels: 93.4 us -> 92.4 us
    pallas_call x1, Pallas kernels: 93.4 us -> 92.4 us  [per_device(): pl.pallas_call(kernel, out_shape=jax.ShapeDtypeStruct((128, D), bf16), in...]
where the time goes in v4:
time: 95.4 us; the launch traced here: 94.9 us
  Pallas kernels  92.4 us (97%)
  local copies, waits for them, and re-layouts  1.88 us (2%)
    pallas_call x1, Pallas kernels, per_device(): pl.pallas_call(kernel, out_shape=jax.ShapeDtypeStruct((128, D), bf16), in...  92.4 us

profile of v4, /device:TPU:2, one launch (start us, length us, event | category | flops | bytes accessed | tf_op | source)
XLA Modules:
  0.0 94.9 jit_solution(5523398522384822658)
XLA Ops:
  0.7 92.4 %shard_map.82 = bf16[128,2048]{1,0:T(8,128)(2,1)} custom-call(bf16[128,2048]{1,0:T(8,128)(2,1)} %tok_ref.1, bf16[2048,384]{1,0:T(8,128)(2,1)} %wq_ref.1, bf16[128,2048]{1,0:T(8,128)(2,1)} %wo_ref.1, f32[1,2048]{1,0:T(1,128)} %shift_ref.1, f32[1,2048]{1,0:T(1,128)} %scale_ref.1, f32[1,2048]{1,0:T(1,128)} %gate_ref.1, s32[1,6]{1,0:T(1,128)} %partners_ref.1, ...), custom_call_target="tpu_custom_call" | custom-call | flops 8000000000 | bytes 30000000 | tf_op jit(solution)/shard_map/pallas_call | solution.py:563
  93.0 1.9 %copy.11 = bf16[128,2048]{1,0:T(8,128)(2,1)} copy(bf16[128,2048]{1,0:T(8,128)(2,1)} %shard_map.82) | data formatting | bytes 1048576

commit v5 on v4

--- a/solution.py
+++ b/solution.py
@@ -60,6 +60,8 @@
     a_r,
     ox_s,
     ox_r,
+    of_s,
+    of_r,
     oy_s,
     oy_r,
     oz_s,
@@ -257,13 +259,20 @@
             wo_ref.at[half_rows], wout.at[c, zl, x, half_rows], ox_s.at[d - 1], ox_r.at[d - 1], x_dev[d]
         )
 
+    def of_copy(i):
+        b = wout.at[c, zl, next_x[3 - 2 * i], quarter_rows(1 - i)]
+        return rcopy(b, b, of_s.at[i], of_r.at[i], x_dev[1 + 2 * i])
+
     def oy_copy(d, up):
         b = wout.at[c, zl, next_x[d], quarter_rows(up)]
         return rcopy(b, b, oy_s.at[d - 1, up], oy_r.at[d - 1, up], y_dev[1 if up else 3])
 
     def drain_w_out():
+        for i in (0, 1):
+            of_copy(i).wait_send()
         for d in range(1, 4):
-            ox_copy(d).wait_send()
+            if d != 2:
+                ox_copy(d).wait_send()
             for up in (1, 0):
                 oy_copy(d, up).wait_send()
 
@@ -279,7 +288,7 @@
         b = wout.at[c, zl] if i == 2 else wout.at[c, 1 - zl, pl.ds(i * 2, 2)]
         return rcopy(b, b, os_s.at[i], os_r.at[i], sib)
 
-    for d in (1, 3, 2):
+    for d in (1, 3):
         ox_copy(d).start()
     pass_weights(1)
     event(1, 0)
@@ -397,12 +406,15 @@
     wait_weights(1)
     wait_weights(2)
     kv_unit(0)
+    for i in (0, 1):
+        ox_copy(1 + 2 * i).wait_recv()
+        of_copy(i).start()
     event(2, 0)
     kv_unit(1)
     kv_unit(7)
     wait_weights(0)
-    for d in range(1, 4):
-        ox_copy(d).wait_recv()
+    for i in (0, 1):
+        of_copy(i).wait_recv()
     for d in range(1, 4):
         for up in (1, 0):
             oy_copy(d, up).start()
@@ -589,6 +601,7 @@
             dma((8, 2)), dma((2, 6)),
             dma((8, 2)), dma((8, 2)),
             dma((3,)), dma((3,)),
+            dma((2,)), dma((2,)),
             dma((3, 2)), dma((3, 2)),
             dma((2,)), dma((2,)),
             dma((2, 2)), dma((2, 2)),

time: 95.4 us -> 95.2 us (level)
  no operation moved by 1% of the time
where the time goes in v5:
time: 95.2 us; the launch traced here: 94.7 us
  Pallas kernels  92.2 us (97%)
  local copies, waits for them, and re-layouts  1.88 us (2%)
    pallas_call x1, Pallas kernels, per_device(): pl.pallas_call(kernel, out_shape=jax.ShapeDtypeStruct((128, D), bf16), in...  92.2 us

profile of v5, /device:TPU:2, one launch (start us, length us, event | category | flops | bytes accessed | tf_op | source)
XLA Modules:
  0.0 94.7 jit_solution(9872719902813314725)
XLA Ops:
  0.7 92.2 %shard_map.82 = bf16[128,2048]{1,0:T(8,128)(2,1)} custom-call(bf16[128,2048]{1,0:T(8,128)(2,1)} %tok_ref.1, bf16[2048,384]{1,0:T(8,128)(2,1)} %wq_ref.1, bf16[128,2048]{1,0:T(8,128)(2,1)} %wo_ref.1, f32[1,2048]{1,0:T(1,128)} %shift_ref.1, f32[1,2048]{1,0:T(1,128)} %scale_ref.1, f32[1,2048]{1,0:T(1,128)} %gate_ref.1, s32[1,6]{1,0:T(1,128)} %partners_ref.1, ...), custom_call_target="tpu_custom_call" | custom-call | flops 8000000000 | bytes 30000000 | tf_op jit(solution)/shard_map/pallas_call | solution.py:575
  92.8 1.9 %copy.11 = bf16[128,2048]{1,0:T(8,128)(2,1)} copy(bf16[128,2048]{1,0:T(8,128)(2,1)} %shard_map.82) | data formatting | bytes 1048576
